TPU v7x, 512 devices: a whole 4x4x16 slice. The times are simulated.
512 devices in a mesh: tm: 32 (over z, core), state: 16 (over y, x).
Axes of the slice: x: 4, y: 4, z: 16, core: 2. Of those that a mesh axis runs over, the one named last changes fastest.
Arguments:
- transition: bfloat16 [32, 1280, 1280], P('tm', 'state'), may hold values from -1 to 1
- covariance: bfloat16 [32, 1280, 1280], P('tm', 'state'), may hold values from -1 to 1, as said below
- information: bfloat16 [32, 1280, 1280], P('tm', 'state'), may hold values from -1 to 1, as said below
- offset_vec: float32 [32, 1280], P('tm', 'state'), may hold values from -6 to 6
- info_vec: float32 [32, 1280], P('tm', 'state'), may hold values from -6 to 6
- step_counts: int32 [32], P('tm'), may hold values from 1 to 8
- scan_level: int32 [1], replicated, may hold values from 0 to 4
Outputs:
- new_trans: bfloat16 [32, 1280, 1280], P('tm', 'state')
- new_covariance: bfloat16 [32, 1280, 1280], P('tm', 'state')
- new_offset: float32 [32, 1280], P('tm', 'state')
- new_counts: int32 [32], P('tm')
Inputs may be any that keep to these rules, and one draw needn't show every extreme that they name: `scan_level`: the partner distance is 2 to this power. `covariance`: each block's matrix is symmetric and positive definite. `information`: each block's matrix is symmetric and positive definite.
All inputs are finite; a program needn't handle non-finite values.
Results may differ from a plain program's by a relative error of at most 0.008.
Values may be sent and summed in bfloat16 or wider, within the bound.
No kernel may reach another device: no remote copies, remote signals or barrier semaphores. Data moves between devices by JAX's collectives and lax.ppermute only.
A program may use at most 64 MiB of HBM per device.

v0:
```python
import jax
import jax.numpy as jnp
from jax import lax
from jax.sharding import PartitionSpec as P


def shortened(array):
    return jax.tree.map(lambda a: a.astype(jnp.bfloat16) if a.dtype == jnp.float32 else a, array)


def from_behind(block, axis, distance):
    devices = range(lax.axis_size(axis))
    route = [(i - distance, i) for i in devices if i - distance in devices]
    return lax.ppermute(block, axis, route)


def fold_rows(left_panel, partial_value, portion):
    left_cols = lax.slice_in_dim(left_panel, 0, portion.shape[0], axis=1)
    return partial_value + jnp.dot(left_cols, portion, preferred_element_type=jnp.float32)


def fetch_at(distance):

    def fetch(operand):
        panels = from_behind((shortened(operand[0]), shortened(operand[1])), "tm", distance)
        vectors = from_behind((operand[2], operand[3]), "tm", distance)
        return (panels[0], panels[1], vectors[0], vectors[1])

    return fetch


def local(transition, covariance, information, offset_vec, info_vec, step_counts, scan_level):
    panel_rows = transition.shape[1]
    full_width = transition.shape[2]
    own_trans = transition[0]
    own_covar = covariance[0]
    own_inform = information[0]
    own_offset = offset_vec[0]
    eta_low = info_vec[0].astype(jnp.bfloat16)
    own_count = step_counts.astype(jnp.float32)
    levels = lax.axis_size("tm").bit_length() - 1
    branches = [fetch_at(2**level_bit) for level_bit in range(levels)]
    part_trans, part_covar, part_offset, part_count = lax.switch(
        scan_level[0], branches, (own_trans, own_covar, own_offset, own_count)
    )
    distance = jnp.left_shift(jnp.int32(1), scan_level[0])
    has_partner = lax.axis_index("tm") >= distance
    start_row = lax.axis_index("state") * panel_rows
    unit_panel = (
        lax.broadcasted_iota(jnp.int32, (panel_rows, full_width), 1)
        == lax.broadcasted_iota(jnp.int32, (panel_rows, full_width), 0) + start_row
    ).astype(jnp.float32)
    guess_scale = 1.0 / (2.0 + 0.4 * (part_count[0] + own_count[0]))
    empty_mat = jnp.zeros((panel_rows, full_width), jnp.float32)
    empty_vec = jnp.zeros((panel_rows,), jnp.float32)
    partial_value = (empty_mat, empty_vec)
    portion = (
        lax.all_gather(own_inform, "state", axis=0, tiled=True),
        lax.all_gather(eta_low, "state", axis=0, tiled=True),
    )
    left_cols = lax.slice_in_dim(part_covar, 0, portion[0].shape[0], axis=1)
    mat_part = partial_value[0] + jnp.dot(left_cols, portion[0], preferred_element_type=jnp.float32)
    vec_part = partial_value[1] + jnp.dot(left_cols, portion[1], preferred_element_type=jnp.float32)
    sum_mat = (unit_panel + mat_part).astype(jnp.bfloat16)
    joined = (part_offset + vec_part).astype(jnp.bfloat16)
    iterate = (
        2.0 * guess_scale * unit_panel - guess_scale * guess_scale * sum_mat.astype(jnp.float32)
    ).astype(jnp.bfloat16)
    for sweep in range(2):
        product = fold_rows(
            sum_mat, empty_mat, lax.all_gather(iterate, "state", axis=0, tiled=True)
        )
        bracket = (2.0 * unit_panel - product).astype(jnp.bfloat16)
        iterate = fold_rows(
            iterate, empty_mat, lax.all_gather(bracket, "state", axis=0, tiled=True)
        ).astype(jnp.bfloat16)
    leading = fold_rows(
        own_trans, empty_mat, lax.all_gather(iterate, "state", axis=0, tiled=True)
    ).astype(jnp.bfloat16)
    partial_value = (empty_mat, empty_mat, empty_vec)
    portion = (
        lax.all_gather(shortened(part_trans), "state", axis=0, tiled=True),
        lax.all_gather(shortened(part_covar), "state", axis=0, tiled=True),
        lax.all_gather(joined, "state", axis=0, tiled=True),
    )
    left_cols = lax.slice_in_dim(leading, 0, portion[0].shape[0], axis=1)
    trans_part = partial_value[0] + jnp.dot(
        left_cols, portion[0], preferred_element_type=jnp.float32
    )
    cov_part = partial_value[1] + jnp.dot(left_cols, portion[1], preferred_element_type=jnp.float32)
    moved_vec = partial_value[2] + jnp.dot(
        left_cols, portion[2], preferred_element_type=jnp.float32
    )
    new_trans = trans_part.astype(jnp.bfloat16)
    right_cov = cov_part.astype(jnp.bfloat16)
    spread = lax.dot_general(
        right_cov,
        lax.all_gather(own_trans, "state", axis=0, tiled=True),
        (((1,), (1,)), ((), ())),
        preferred_element_type=jnp.float32,
    )
    new_covariance = (spread + own_covar.astype(jnp.float32)).astype(jnp.bfloat16)
    new_offset = moved_vec + own_offset
    new_trans = jnp.where(has_partner, new_trans, own_trans)
    new_covariance = jnp.where(has_partner, new_covariance, own_covar)
    new_offset = jnp.where(has_partner, new_offset, own_offset)
    new_counts = jnp.where(has_partner, part_count + own_count, own_count).astype(jnp.int32)
    return (new_trans[None], new_covariance[None], new_offset[None], new_counts)


def solution(mesh):
    in_specs = (
        P("tm", "state", None),
        P("tm", "state", None),
        P("tm", "state", None),
        P("tm", "state"),
        P("tm", "state"),
        P("tm"),
        P(),
    )
    out_specs = (P("tm", "state", None), P("tm", "state", None), P("tm", "state"), P("tm"))
    return jax.shard_map(local, mesh=mesh, in_specs=in_specs, out_specs=out_specs, check_vma=False)
```

profile of v0, /device:TPU:1, one launch (start us, length us, event | category | flops | bytes accessed | tf_op | source)
XLA Modules:
  0.0 620.3 jit_solution(2651580521094980330)
XLA Ops:
  9.2 23.6 %conditional.1 = (bf16[80,1280]{1,0:T(8,128)(2,1)}, bf16[80,1280]{1,0:T(8,128)(2,1)}, f32[80]{0:T(128)}, f32[1]{0:T(128)}) conditional(s32[]{:T(128)} %bitcast.1, (bf16[80,1280]{1,0:T(8,128)(2,1)}, bf16[80,1280]{1,0:T(8,128)(2,1)}, f32[80]{0:T(128)}, f32[1]{0:T(128)}) %tuple.86, (bf16[80,1280]{1,0:T(8,128)(2,1)}, ...), branch_computations={%region_0.0_spmd, %region_1.0_spmd, %region_2.0_spmd, %region_3.0_... | conditional | bytes 1639888 | solution.py:43
  9.3 6.4 %collective-permute-start.8 = (bf16[80,1280]{1,0:T(8,128)(2,1)}, bf16[80,1280]{1,0:T(8,128)(2,1)}, u32[]{:S(2)}, u32[]{:S(2)}) collective-permute-start(bf16[80,1280]{1,0:T(8,128)(2,1)} %get-tuple-element.58), channel_id=1, source_target_pairs={{0,64},{16,80},{32,96},{48,112},{64,128},{80,144},{96,160},{112,17... | collective-permute-start | bytes 614408 | tf_op jit(solution)/shard_map/cond/branch_2_fun/ppermute | solution.py:14
  15.7 6.1 collective-permute-start.9
  21.8 4.8 collective-permute-start.10
  26.6 6.2 %collective-permute-start.11 = (f32[1]{0:T(128)}, f32[1]{0:T(128)}, u32[]{:S(2)}, u32[]{:S(2)}) collective-permute-start(f32[1]{0:T(128)} %get-tuple-element.61), channel_id=1, source_target_pairs={{0,64},{16,80},{32,96},{48,112},{64,128},{80,144},{96,160},{112,17... | collective-permute-start | bytes 20 | tf_op jit(solution)/shard_map/cond/branch_2_fun/ppermute | solution.py:14
  33.5 46.2 %all-gather.27.cloned.1.call-done = bf16[1,1280,1280]{2,1,0:T(8,128)(2,1)} async-done(((bf16[1,80,1280]{2,1,0:T(8,128)(2,1)}), bf16[1,1280,1280]{2,1,0:T(8,128)(2,1)}) %all-gather.27.cloned.1.call-update) | async-done | bytes 3276816 | tf_op jit(solution)/shard_map/all_gather | solution.py:58
  79.7 3.4 subtract_convert_fusion
  83.2 62.7 %all-gather.13.cloned.1.call-done = bf16[1280,1280]{1,0:T(8,128)(2,1)} async-done(((bf16[80,1280]{1,0:T(8,128)(2,1)}), bf16[1280,1280]{1,0:T(8,128)(2,1)}) %all-gather.13.cloned.1.call-update) | async-done | bytes 3276816 | tf_op jit(solution)/shard_map/all_gather | solution.py:71
  145.9 3.3 fusion.10
  149.3 62.8 %all-gather.15.cloned.1.call-done = bf16[1280,1280]{1,0:T(8,128)(2,1)} async-done(((bf16[80,1280]{1,0:T(8,128)(2,1)}), bf16[1280,1280]{1,0:T(8,128)(2,1)}) %all-gather.15.cloned.1.call-update) | async-done | bytes 3276816 | tf_op jit(solution)/shard_map/all_gather | solution.py:75
  212.1 3.3 convolution_convert_fusion.4
  215.5 62.7 %all-gather.17.cloned.1.call-done = bf16[1280,1280]{1,0:T(8,128)(2,1)} async-done(((bf16[80,1280]{1,0:T(8,128)(2,1)}), bf16[1280,1280]{1,0:T(8,128)(2,1)}) %all-gather.17.cloned.1.call-update) | async-done | bytes 3276816 | tf_op jit(solution)/shard_map/all_gather | solution.py:71
  278.2 3.3 fusion.11
  281.6 62.7 %all-gather.19.cloned.1.call-done = bf16[1280,1280]{1,0:T(8,128)(2,1)} async-done(((bf16[80,1280]{1,0:T(8,128)(2,1)}), bf16[1280,1280]{1,0:T(8,128)(2,1)}) %all-gather.19.cloned.1.call-update) | async-done | bytes 3276816 | tf_op jit(solution)/shard_map/all_gather | solution.py:75
  344.3 3.3 convolution_convert_fusion.3
  349.9 1.3 dynamic-slice
  352.1 31.1 %all-reduce = bf16[1280]{0:T(1024)(128)(2,1)S(1)} all-reduce(bf16[1280]{0:T(1024)(128)(2,1)S(1)} %dynamic-update-slice), channel_id=4, replica_groups=mesh['tm'=32,'state'=16] {'state'}, use_global_device_ids=true, to_apply=%add | all-reduce | flops 1280 | bytes 5120 | tf_op jit(solution)/shard_map/all_gather | solution.py:59
  384.5 28.7 %all-reduce.1 = bf16[1280]{0:T(1024)(128)(2,1)S(1)} all-reduce(bf16[1280]{0:T(1024)(128)(2,1)S(1)} %dynamic-update-slice.1), channel_id=1, replica_groups=mesh['tm'=32,'state'=16] {'state'}, use_global_device_ids=true, to_apply=%add.1 | all-reduce | flops 1280 | bytes 5120
  413.3 2.7 convolution_convert_fusion
  416.7 59.5 %all-gather.23.cloned.1.call-done = bf16[1280,1280]{1,0:T(8,128)(2,1)} async-done(((bf16[80,1280]{1,0:T(8,128)(2,1)}), bf16[1280,1280]{1,0:T(8,128)(2,1)}) %all-gather.23.cloned.1.call-update) | async-done | bytes 3276816 | tf_op jit(solution)/shard_map/all_gather | solution.py:82
  476.2 3.3 fusion.25
  479.5 62.3 %all-gather.25.cloned.1.call-done = bf16[1280,1280]{1,0:T(8,128)(2,1)} async-done(((bf16[80,1280]{1,0:T(8,128)(2,1)}), bf16[1280,1280]{1,0:T(8,128)(2,1)}) %all-gather.25.cloned.1.call-update) | async-done | bytes 3276816 | tf_op jit(solution)/shard_map/all_gather | solution.py:83
  541.8 65.6 %all-gather.29.cloned.1.call-done = bf16[1,1280,1280]{2,1,0:T(8,128)(2,1)} async-done(((bf16[1,80,1280]{2,1,0:T(8,128)(2,1)}), bf16[1,1280,1280]{2,1,0:T(8,128)(2,1)}) %all-gather.29.cloned.1.call-update) | async-done | bytes 3276816 | tf_op jit(solution)/shard_map/all_gather | solution.py:98
  607.4 5.2 fusion.22
  (45 shorter events, 5.6 us)
Async XLA Ops:
  7.2 72.5 %all-gather.27.cloned.1.call-start = ((), (), s32[]{:S(2)}) async-start(), calls=%async_computation.7 | async-start | bytes 3481600 | tf_op jit(solution)/shard_map/all_gather | solution.py:58
  7.9 138.0 %all-gather.13.cloned.1.call-start = ((), (), s32[]{:S(2)}) async-start(), calls=%async_computation | async-start | bytes 3481600 | tf_op jit(solution)/shard_map/all_gather | solution.py:71
  9.3 23.6 %collective-permute-start.8 = (bf16[80,1280]{1,0:T(8,128)(2,1)}, bf16[80,1280]{1,0:T(8,128)(2,1)}, u32[]{:S(2)}, u32[]{:S(2)}) collective-permute-start(bf16[80,1280]{1,0:T(8,128)(2,1)} %get-tuple-element.58), channel_id=1, source_target_pairs={{0,64},{16,80},{32,96},{48,112},{64,128},{80,144},{96,160},{112,17... | collective-permute-start | bytes 614408 | tf_op jit(solution)/shard_map/cond/branch_2_fun/ppermute | solution.py:14
  15.7 17.2 %collective-permute-start.9 = (bf16[80,1280]{1,0:T(8,128)(2,1)}, bf16[80,1280]{1,0:T(8,128)(2,1)}, u32[]{:S(2)}, u32[]{:S(2)}) collective-permute-start(bf16[80,1280]{1,0:T(8,128)(2,1)} %get-tuple-element.59), channel_id=1, source_target_pairs={{0,64},{16,80},{32,96},{48,112},{64,128},{80,144},{96,160},{112,17... | collective-permute-start | bytes 614408 | tf_op jit(solution)/shard_map/cond/branch_2_fun/ppermute | solution.py:14
  21.8 11.1 %collective-permute-start.10 = (f32[80]{0:T(128)}, f32[80]{0:T(128)}, u32[]{:S(2)}, u32[]{:S(2)}) collective-permute-start(f32[80]{0:T(128)} %get-tuple-element.60), channel_id=1, source_target_pairs={{0,64},{16,80},{32,96},{48,112},{64,128},{80,144},{96,160},{112,17... | collective-permute-start | bytes 968 | tf_op jit(solution)/shard_map/cond/branch_2_fun/ppermute | solution.py:14
  26.6 6.2 %collective-permute-start.11 = (f32[1]{0:T(128)}, f32[1]{0:T(128)}, u32[]{:S(2)}, u32[]{:S(2)}) collective-permute-start(f32[1]{0:T(128)} %get-tuple-element.61), channel_id=1, source_target_pairs={{0,64},{16,80},{32,96},{48,112},{64,128},{80,144},{96,160},{112,17... | collective-permute-start | bytes 20 | tf_op jit(solution)/shard_map/cond/branch_2_fun/ppermute | solution.py:14
  83.1 129.0 %copy-start.2 = (bf16[80,1280]{1,0:T(8,128)(2,1)S(1)}, bf16[80,1280]{1,0:T(8,128)(2,1)}, u32[]{:S(2)}) copy-start(bf16[80,1280]{1,0:T(8,128)(2,1)} %get-tuple-element.82) | copy-start | bytes 614404
  83.2 129.0 %all-gather.15.cloned.1.call-start = ((), (), s32[]{:S(2)}) async-start(), calls=%async_computation.1 | async-start | bytes 3481600 | tf_op jit(solution)/shard_map/all_gather | solution.py:75
  149.3 129.0 %all-gather.17.cloned.1.call-start = ((), (), s32[]{:S(2)}) async-start(), calls=%async_computation.2 | async-start | bytes 3481600 | tf_op jit(solution)/shard_map/all_gather | solution.py:71
  215.4 128.9 %copy-start = (bf16[80,1280]{1,0:T(8,128)(2,1)S(1)}, bf16[80,1280]{1,0:T(8,128)(2,1)}, u32[]{:S(2)}) copy-start(bf16[80,1280]{1,0:T(8,128)(2,1)} %convolution_convert_fusion.4) | copy-start | bytes 614404
  215.5 128.8 %all-gather.19.cloned.1.call-start = ((), (), s32[]{:S(2)}) async-start(), calls=%async_computation.3 | async-start | bytes 3481600 | tf_op jit(solution)/shard_map/all_gather | solution.py:75
  281.5 70.3 %copy-start.4 = (f32[1,80]{1,0:T(1,128)S(1)}, f32[1,80]{1,0:T(1,128)}, u32[]{:S(2)}) copy-start(f32[1,80]{1,0:T(1,128)} %param.16) | copy-start | bytes 964
  281.5 131.8 %copy-start.1 = (bf16[1,80,1280]{2,1,0:T(8,128)(2,1)S(1)}, bf16[1,80,1280]{2,1,0:T(8,128)(2,1)}, u32[]{:S(2)}) copy-start(bf16[1,80,1280]{2,1,0:T(8,128)(2,1)} %param.12) | copy-start | bytes 614404
  281.5 131.7 %all-gather.21.cloned.1.call-start = ((), (), s32[]{:S(2)}) async-start(), calls=%async_computation.4 | async-start | bytes 3481600 | tf_op jit(solution)/shard_map/all_gather | solution.py:78
  347.6 68.4 %copy-start.5 = (f32[1,80]{1,0:T(1,128)S(1)}, f32[1,80]{1,0:T(1,128)}, u32[]{:S(2)}) copy-start(f32[1,80]{1,0:T(1,128)} %param.15) | copy-start | bytes 964
  347.6 128.5 %all-gather.23.cloned.1.call-start = ((), (), s32[]{:S(2)}) async-start(), calls=%async_computation.5 | async-start | bytes 3481600 | tf_op jit(solution)/shard_map/all_gather | solution.py:82
  348.4 193.4 %all-gather.25.cloned.1.call-start = ((), (), s32[]{:S(2)}) async-start(), calls=%async_computation.6 | async-start | bytes 3481600 | tf_op jit(solution)/shard_map/all_gather | solution.py:83
  349.1 258.3 %all-gather.29.cloned.1.call-start = ((), (), s32[]{:S(2)}) async-start(), calls=%async_computation.8 | async-start | bytes 3481600 | tf_op jit(solution)/shard_map/all_gather | solution.py:98
  413.3 194.2 %copy-start.3 = (bf16[1,80,1280]{2,1,0:T(8,128)(2,1)S(1)}, bf16[1,80,1280]{2,1,0:T(8,128)(2,1)}, u32[]{:S(2)}) copy-start(bf16[1,80,1280]{2,1,0:T(8,128)(2,1)} %param.13) | copy-start | bytes 614404
Sparse Core Ops, SparseCore 0:
  11.0 68.6 all-gather.26
  83.3 62.5 all-gather.12
  149.5 62.5 all-gather.14
  215.6 62.5 all-gather.16
  281.7 62.5 all-gather.18
  347.7 62.7 all-gather.20
  413.5 62.5 all-gather.22
  479.2 62.5 all-gather.24
  544.8 62.5 all-gather.28
where the time goes:
time: 621 us; the launch traced here: 620 us
  waiting for transfers between devices  487 us (78%)
  blocking collectives  59.8 us (10%)
  matrix products  29.6 us (5%)
  starting transfers between devices  23.9 us (4%)
  between operations  17.6 us (3%)
    all_gather x2, waiting for transfers between devices, local(): lax.all_gather(bracket, 'state', axis=0, tiled=True)  126 us
    all_gather x3, waiting for transfers between devices, local(): lax.all_gather(iterate, 'state', axis=0, tiled=True)  125 us
    all_gather x1, waiting for transfers between devices, local(): lax.all_gather(own_trans, 'state', axis=0, tiled=True)  65.6 us
    all_gather x1, waiting for transfers between devices, local(): lax.all_gather(shortened(part_covar), 'state', axis=0, tiled=True)  62.3 us
    all_gather x1, waiting for transfers between devices, local(): lax.all_gather(shortened(part_trans), 'state', axis=0, tiled=True)  59.5 us
    all_gather x1, waiting for transfers between devices, local(): lax.all_gather(own_inform, 'state', axis=0, tiled=True)  46.2 us
    all_gather x1, blocking collectives, local(): lax.all_gather(eta_low, 'state', axis=0, tiled=True)  31.1 us
    unnamed x1, blocking collectives  28.7 us
  transfers between devices with their start and end apart: 13, of which 8 were waited for; matrix products, arithmetic and copies ran while one was open for 2% of the time, Pallas kernels for 0%

commit v1 on v0

v1 whole, which is shorter than its diff:
```python
import functools
import jax
import jax.numpy as jnp
from jax import lax
from jax.experimental import pallas as pl
from jax.experimental.pallas import tpu as pltpu
from jax.sharding import PartitionSpec as P

F32, BF16 = jnp.float32, jnp.bfloat16
VEC_ROWS = 16
LANES = 128
STRIP = 256


def matmul(a, b):
    return jnp.dot(a, b, preferred_element_type=F32)


def combine_kernel(
    rows, shards,
    scale_ref, trans_ref, covar_ref, gathered,
    trans_out, covar_out, moved_out,
    inform, pcovar, ptrans, otrans, vectors, ratio, panel, joined, sems,
):
    width = trans_ref.shape[1]
    strips = width // STRIP
    wide = vectors.shape[2]
    homes = (inform, pcovar, ptrans, otrans)
    copies = []
    for k, home in enumerate(homes):
        copies.append(pltpu.make_async_copy(gathered.at[:, pl.ds(k * rows, rows), :], home, sems.at[k]))
    copies.append(pltpu.make_async_copy(gathered.at[:, pl.ds(4 * rows, VEC_ROWS), :], vectors, sems.at[4]))
    for k in (0, 1, 4, 2, 3):
        copies[k].start()
    copies[0].wait()
    copies[1].wait()
    scale = scale_ref[0]
    tall = width // 2

    @pl.loop(0, strips)
    def _(s):
        cols = pl.ds(pl.multiple_of(s * STRIP, STRIP), STRIP)
        right = inform[:, :, cols].reshape(width, STRIP)
        for half in range(2):
            left = pcovar[pl.ds(half * shards // 2, shards // 2)].reshape(tall, width)
            unit = (
                lax.broadcasted_iota(jnp.int32, (tall, STRIP), 0) + half * tall
                == lax.broadcasted_iota(jnp.int32, (tall, STRIP), 1) + s * STRIP
            ).astype(F32)
            sum_mat = (unit + matmul(left, right)).astype(BF16).astype(F32)
            ratio[pl.ds(half * tall, tall), cols] = (unit - scale * sum_mat).astype(BF16)

    panel[0] = trans_ref[...]
    for step in range(7):
        now, later = step % 2, (step + 1) % 2
        last = step == 6

        @pl.loop(0, strips)
        def _(s):
            cols = pl.ds(pl.multiple_of(s * STRIP, STRIP), STRIP)
            value = trans_ref[:, cols].astype(F32) + matmul(panel[now], ratio[:, cols])
            if last:
                value = value * scale
            panel[later, :, cols] = value.astype(BF16)

    copies[4].wait()
    eta, offset = [], []
    packed = vectors[...]
    lane = lax.broadcasted_iota(jnp.int32, (rows, wide // (rows // VEC_ROWS)), 1)
    block = wide // (rows // VEC_ROWS)
    for q in range(shards):
        pieces = [packed[q][:, pl_k * block:(pl_k + 1) * block] for pl_k in range(rows // VEC_ROWS)]
        whole = jnp.concatenate(pieces, axis=0)
        offset.append(
            jnp.sum(jnp.where((lane >= 1) & (lane <= 3), whole.astype(F32), 0.0), axis=1, keepdims=True)
        )
        joined[pl.ds(q * rows, rows), :] = jnp.where(lane == 0, whole.astype(F32), 0.0).astype(BF16)
    eta = joined[...]
    for half in range(2):
        left = pcovar[pl.ds(half * shards // 2, shards // 2)].reshape(tall, width)
        moved = matmul(left, eta)
        base = jnp.concatenate(offset[half * shards // 2:(half + 1) * shards // 2], axis=0)
        lane_t = lax.broadcasted_iota(jnp.int32, (tall, block), 1)
        joined[pl.ds(half * tall, tall), :] = jnp.where(lane_t == 0, moved + base, 0.0).astype(BF16)
    moved_out[...] = matmul(panel[1], joined[...])

    copies[2].wait()

    @pl.loop(0, strips)
    def _(s):
        cols = pl.ds(pl.multiple_of(s * STRIP, STRIP), STRIP)
        right = pcovar[:, :, cols].reshape(width, STRIP)
        panel[0, :, cols] = matmul(panel[1], right).astype(BF16)
        trans_out[:, cols] = matmul(panel[1], ptrans[:, :, cols].reshape(width, STRIP)).astype(BF16)

    copies[3].wait()
    moved = lax.dot_general(
        panel[0], otrans[...].reshape(width, width), (((1,), (1,)), ((), ())), preferred_element_type=F32
    )
    covar_out[...] = (moved + covar_ref[...].astype(F32)).astype(BF16)


def combine(scale, trans, covar, gathered):
    rows, width = trans.shape
    shards = gathered.shape[0]
    block = width // (rows // VEC_ROWS)
    vmem = pl.BlockSpec(memory_space=pltpu.VMEM)
    mat = pltpu.VMEM((shards, rows, width), BF16)
    return pl.pallas_call(
        functools.partial(combine_kernel, rows, shards),
        out_shape=(
            jax.ShapeDtypeStruct((rows, width), BF16),
            jax.ShapeDtypeStruct((rows, width), BF16),
            jax.ShapeDtypeStruct((rows, block), F32),
        ),
        in_specs=[pl.BlockSpec(memory_space=pltpu.SMEM), vmem, vmem, pl.BlockSpec(memory_space=pl.ANY)],
        out_specs=(vmem, vmem, vmem),
        scratch_shapes=[
            mat, mat, mat, mat,
            pltpu.VMEM((shards, VEC_ROWS, width), BF16),
            pltpu.VMEM((width, width), BF16),
            pltpu.VMEM((2, rows, width), BF16),
            pltpu.VMEM((width, block), BF16),
            pltpu.SemaphoreType.DMA((5,)),
        ],
        compiler_params=pltpu.CompilerParams(vmem_limit_bytes=48 * 2**20),
        name="combine",
    )(scale, trans, covar, gathered)


def spread_vectors(columns, rows, width):
    parts = rows // VEC_ROWS
    block = width // parts
    stacked = jnp.stack(columns, axis=1)
    whole = jnp.pad(stacked, ((0, 0), (0, block - stacked.shape[1])))
    return whole.reshape(parts, VEC_ROWS, block).transpose(1, 0, 2).reshape(VEC_ROWS, width)


def thirds(vector):
    high = vector.astype(BF16)
    rest = vector - high.astype(F32)
    middle = rest.astype(BF16)
    low = (rest - middle.astype(F32)).astype(BF16)
    return high, middle, low


def from_behind(block, axis, distance):
    devices = range(lax.axis_size(axis))
    route = [(i - distance, i) for i in devices if i - distance in devices]
    return lax.ppermute(block, axis, route)


def local(transition, covariance, information, offset_vec, info_vec, step_counts, scan_level):
    rows, width = transition.shape[1:]
    trans, covar, inform = transition[0], covariance[0], information[0]
    offset = offset_vec[0]
    count = step_counts.astype(F32)
    nothing = jnp.zeros((rows,), BF16)
    high, middle, low = thirds(offset)
    counts = jnp.broadcast_to(count.astype(BF16), (rows,))
    sent_vectors = spread_vectors([nothing, high, middle, low, counts], rows, width)
    own_vectors = spread_vectors([info_vec[0].astype(BF16)], rows, width)
    sent = jnp.concatenate([covar, trans, sent_vectors], axis=0)
    levels = lax.axis_size("tm").bit_length() - 1
    branches = [functools.partial(from_behind, axis="tm", distance=2**k) for k in range(levels)]
    got = lax.switch(scan_level[0], branches, sent)
    part_count = got[2 * rows, 4:5].astype(F32)
    scale = 1.0 / (2.0 + 0.4 * (part_count + count))
    packed = jnp.concatenate(
        [inform, got[: 2 * rows], trans, got[2 * rows :] + own_vectors], axis=0
    )
    gathered = lax.all_gather(packed, "state", axis=0, tiled=False)
    new_trans, new_covariance, moved = combine(scale, trans, covar, gathered)
    new_offset = moved[:, 0] + offset
    distance = jnp.left_shift(jnp.int32(1), scan_level[0])
    has_partner = lax.axis_index("tm") >= distance
    new_trans = jnp.where(has_partner, new_trans, trans)
    new_covariance = jnp.where(has_partner, new_covariance, covar)
    new_offset = jnp.where(has_partner, new_offset, offset)
    new_counts = jnp.where(has_partner, part_count + count, count).astype(jnp.int32)
    return (new_trans[None], new_covariance[None], new_offset[None], new_counts)


def solution(mesh):
    in_specs = (
        P("tm", "state", None),
        P("tm", "state", None),
        P("tm", "state", None),
        P("tm", "state"),
        P("tm", "state"),
        P("tm"),
        P(),
    )
    out_specs = (P("tm", "state", None), P("tm", "state", None), P("tm", "state"), P("tm"))
    return jax.shard_map(local, mesh=mesh, in_specs=in_specs, out_specs=out_specs, check_vma=False)
```

time: 621 us -> 215 us (0.35)
  waiting for transfers between devices: 487 us -> 149 us
  blocking collectives: 59.8 us -> 0 us
  matrix products: 29.6 us -> 0 us
  Pallas kernels: 0 us -> 22.8 us
  starting transfers between devices: 23.9 us -> 17.1 us
  other arithmetic: 0.01 us -> 6.24 us
    all_gather x9 -> x1, waiting for transfers between devices: 485 us -> 141 us  [local(): gathered = lax.all_gather(packed, 'state', axis=0, tiled=False)]
    all_gather x1 -> x0, blocking collectives: 31.1 us -> none  [local(): lax.all_gather(eta_low, 'state', axis=0, tiled=True)]
    dot_general x10 -> x0, matrix products: 29.6 us -> none  [the longest x5 15.9 us: fold_rows(): jnp.dot(left_cols, portion, preferred_element_type=jnp.float32)]
    unnamed x1 -> x0, blocking collectives: 28.7 us -> none
    pallas_call x0 -> x1, Pallas kernels: none -> 22.8 us  [combine(): pl.pallas_call(functools.partial(combine_kernel, rows, shards), out_shape...]
    ppermute x4 -> x1, waiting for transfers between devices: 0.01 us -> 8.21 us  [from_behind(): return lax.ppermute(block, axis, route)]
    ppermute x4 -> x1, starting transfers between devices: 23.6 us -> 17.1 us  [from_behind(): return lax.ppermute(block, axis, route)]
  transfers between devices with their start and end apart: 13 -> 2, of which waited for: 8 -> 2; matrix products, arithmetic and copies ran while one was open for 2% -> 1% of each run, Pallas kernels for 0% -> 0%
where the time goes in v1:
time: 215 us
  waiting for transfers between devices  149 us (69%)
  Pallas kernels  22.8 us (11%)
  between operations  17.3 us (8%)
  starting transfers between devices  17.1 us (8%)
  other arithmetic  6.24 us (3%)
  local copies, waits for them, and re-layouts  2.76 us (1%)
    all_gather x1, waiting for transfers between devices, local(): gathered = lax.all_gather(packed, 'state', axis=0, tiled=False)  141 us
    pallas_call x1, Pallas kernels, combine(): pl.pallas_call(functools.partial(combine_kernel, rows, shards), out_shape...  22.8 us
    ppermute x1, starting transfers between devices, from_behind(): return lax.ppermute(block, axis, route)  17.1 us
    ppermute x1, waiting for transfers between devices, from_behind(): return lax.ppermute(block, axis, route)  8.21 us
  transfers between devices with their start and end apart: 2, of which 2 were waited for; matrix products, arithmetic and copies ran while one was open for 1% of the time, Pallas kernels for 0%

profile of v1, /device:TPU:1, one launch (start us, length us, event | category | flops | bytes accessed | tf_op | source)
XLA Modules:
  0.0 215.2 jit_solution(16057253611575397084)
XLA Ops:
  7.2 0.0 copy-start
  7.2 0.0 copy-start.2
  7.2 0.0 all-gather.3.cloned.1.call-start
  7.2 0.8 bitcast_convert_fusion
  8.0 0.7 subtract_convert_fusion
  9.9 0.7 convert_bitcast_fusion
  10.7 0.1 copy.17
  10.8 0.1 copy.18
  10.9 1.1 pad_maximum_fusion.1
  12.0 25.3 %conditional.1 = (bf16[176,1280]{1,0:T(8,128)(2,1)}) conditional(s32[]{:T(128)} %bitcast.1, bf16[176,1280]{1,0:T(8,128)(2,1)S(1)} %pad_maximum_fusion.1, bf16[176,1280]{1,0:T(8,128)(2,1)S(1)} %pad_maximum_fusion.1, bf16[176,1280]{1,0:T(8,128)(2,1)S(1)} %pad_maximum_fusion.1, ...), branch_computations={%region_0.1_spmd, %region_1.2_spmd, %region_2.3_spmd, %region_3.4_... | conditional | bytes 1802288 | solution.py:166
  12.0 17.1 %collective-permute-start.4 = (bf16[176,1280]{1,0:T(8,128)(2,1)S(1)}, bf16[176,1280]{1,0:T(8,128)(2,1)}, u32[]{:S(2)}, u32[]{:S(2)}) collective-permute-start(bf16[176,1280]{1,0:T(8,128)(2,1)S(1)} %param.4), channel_id=1, source_target_pairs={{0,256},{16,272},{32,288},{48,304},{64,320},{80,336},{96,352},{112... | collective-permute-start | bytes 1351688 | tf_op jit(solution)/shard_map/cond/branch_4_fun/ppermute | solution.py:150
  29.1 8.2 %collective-permute-done.4 = bf16[176,1280]{1,0:T(8,128)(2,1)} collective-permute-done((bf16[176,1280]{1,0:T(8,128)(2,1)S(1)}, bf16[176,1280]{1,0:T(8,128)(2,1)}, u32[]{:S(2)}, u32[]{:S(2)}) %collective-permute-start.4) | collective-permute-done | bytes 450592 | tf_op jit(solution)/shard_map/cond/branch_4_fun/ppermute | solution.py:150
  37.3 1.1 slice.17
  38.4 0.8 slice_add_fusion
  39.2 0.0 copy-done
  39.2 0.0 copy-done.2
  39.2 1.0 pad_maximum_fusion
  40.2 0.0 all-gather.3.cloned.1.call-update
  40.2 1.3 slice.16
  42.1 140.8 %all-gather.3.cloned.1.call-done = bf16[5376,1280]{1,0:T(8,128)(2,1)} async-done(((bf16[336,1280]{1,0:T(8,128)(2,1)}), bf16[5376,1280]{1,0:T(8,128)(2,1)}) %all-gather.3.cloned.1.call-update) | async-done | bytes 13762576 | tf_op jit(solution)/shard_map/all_gather | solution.py:172
  182.9 22.8 %combine.1 = (bf16[80,1280]{1,0:T(8,128)(2,1)S(1)}, bf16[80,1280]{1,0:T(8,128)(2,1)S(1)}, f32[80,256]{1,0:T(8,128)S(1)}) custom-call(f32[1]{0:T(128)S(6)} %div.3.scale_ref, bf16[80,1280]{1,0:T(8,128)(2,1)S(1)} %bitcast.45, bf16[80,1280]{1,0:T(8,128)(2,1)S(1)} %bitcast.47, bf16[16,336,1280]{2,1,0:T(8,128)(2,1)} %bitcast.48), custom_call_target="tpu_custom_call" | custom-call | tf_op jit(solution)/shard_map/combine/pallas_call | solution.py:109
  205.7 0.1 slice_reduce_fusion
  205.9 0.5 broadcast_select_fusion
  206.4 0.8 select_bitcast_fusion
  (11 shorter events, 0.1 us)
Async XLA Ops:
  7.2 32.0 %copy-start = (bf16[1,80,1280]{2,1,0:T(8,128)(2,1)S(1)}, bf16[1,80,1280]{2,1,0:T(8,128)(2,1)}, u32[]{:S(2)}) copy-start(bf16[1,80,1280]{2,1,0:T(8,128)(2,1)} %param.12) | copy-start | bytes 614404
  7.2 32.0 %copy-start.2 = (bf16[1,80,1280]{2,1,0:T(8,128)(2,1)S(1)}, bf16[1,80,1280]{2,1,0:T(8,128)(2,1)}, u32[]{:S(2)}) copy-start(bf16[1,80,1280]{2,1,0:T(8,128)(2,1)} %param.14) | copy-start | bytes 614404
  7.2 175.7 %all-gather.3.cloned.1.call-start = ((), (), s32[]{:S(2)}) async-start(), calls=%async_computation | async-start | bytes 14622720 | tf_op jit(solution)/shard_map/all_gather | solution.py:172
  12.0 25.3 %collective-permute-start.4 = (bf16[176,1280]{1,0:T(8,128)(2,1)S(1)}, bf16[176,1280]{1,0:T(8,128)(2,1)}, u32[]{:S(2)}, u32[]{:S(2)}) collective-permute-start(bf16[176,1280]{1,0:T(8,128)(2,1)S(1)} %param.4), channel_id=1, source_target_pairs={{0,256},{16,272},{32,288},{48,304},{64,320},{80,336},{96,352},{112... | collective-permute-start | bytes 1351688 | tf_op jit(solution)/shard_map/cond/branch_4_fun/ppermute | solution.py:150
  37.3 145.6 %copy-start.1 = (bf16[1,80,1280]{2,1,0:T(8,128)(2,1)S(1)}, bf16[1,80,1280]{2,1,0:T(8,128)(2,1)}, u32[]{:S(2)}) copy-start(bf16[1,80,1280]{2,1,0:T(8,128)(2,1)} %param.13) | copy-start | bytes 614404
  182.9 22.9 %copy-start.3 = (f32[1,80]{1,0:T(1,128)S(1)}, f32[1,80]{1,0:T(1,128)}, u32[]{:S(2)}) copy-start(f32[1,80]{1,0:T(1,128)} %param.15) | copy-start | bytes 964
Sparse Core Ops, SparseCore 0:
  40.3 142.5 all-gather.2

commit v2 on v0

v2 whole, which is shorter than its diff:
```python
import jax
import jax.numpy as jnp
from jax import lax
from jax.experimental import pallas as pl
from jax.experimental.pallas import tpu as pltpu
from jax.sharding import PartitionSpec as P

F32, BF16, F16 = jnp.float32, jnp.bfloat16, jnp.float16
NOTE_ROWS = 16
STRIP = 256
BASE = 2.0**12
STEP = 2.0**16
STEPS = 7
ETA, ETA_GRADE, INFORM_GRADE, OWN_TRANS_GRADE = 0, 1, 2, 3
OFFSET, OFFSET_GRADE, COVAR_GRADE, TRANS_GRADE, COUNT = 4, 7, 8, 9, 10

VMEM = pl.BlockSpec(memory_space=pltpu.VMEM)
SMEM = pl.BlockSpec(memory_space=pltpu.SMEM)
ANY = pl.BlockSpec(memory_space=pl.ANY)


def matmul(a, b):
    return jnp.dot(a, b, preferred_element_type=F32)


def times_transpose(a, b):
    return lax.dot_general(a, b, (((1,), (1,)), ((), ())), preferred_element_type=F32)


def graded(value):
    peak = jnp.max(jnp.max(jnp.abs(value), axis=1, keepdims=True), axis=0, keepdims=True)
    factor, grade = jnp.full((1, 1), BASE, F32), jnp.zeros((1, 1), F32)
    for k in range(1, STEPS + 1):
        small = peak < STEP**-k
        factor = jnp.where(small, factor * STEP, factor)
        grade = jnp.where(small, grade + 1.0, grade)
    return factor, grade


def inverse(grade):
    factor = jnp.full(grade.shape, 1.0 / BASE, F32)
    for k in range(1, STEPS + 1):
        factor = jnp.where(grade >= k, factor * (1.0 / STEP), factor)
    return factor


def pack_kernel(trans_ref, covar_ref, inform_ref, offset_ref, eta_ref, count_ref, sent_ref, own_ref):
    rows, width = trans_ref.shape

    def put(target, first, value_ref):
        value = value_ref[...].astype(F32)
        factor, grade = graded(value)
        target[first : first + rows, :] = (value * factor).astype(BF16)
        return jnp.broadcast_to(grade, (1, rows))

    covar_grade = put(sent_ref, 0, covar_ref)
    trans_grade = put(sent_ref, rows, trans_ref)
    inform_grade = put(own_ref, 0, inform_ref)
    own_ref[rows : 2 * rows, :] = sent_ref[rows : 2 * rows, :]
    eta = eta_ref[...].astype(BF16).astype(F32)
    eta_factor, eta_grade = graded(eta)
    offset = offset_ref[...]
    offset_factor, offset_grade = graded(offset)
    offset = offset * offset_factor
    parts = []
    for _ in range(3):
        part = offset.astype(BF16).astype(F32)
        parts.append(part)
        offset = offset - part
    one = jnp.ones((1, rows), F32)
    own_notes = [eta * eta_factor, one * eta_grade, inform_grade, trans_grade]
    count = one * count_ref[0].astype(F32)
    sent_notes = parts + [one * offset_grade, covar_grade, trans_grade, count]

    def notes(first, given):
        index = lax.broadcasted_iota(jnp.int32, (NOTE_ROWS, rows), 0)
        total = jnp.zeros((NOTE_ROWS, rows), F32)
        for k, row in enumerate(given):
            total = jnp.where(index == first + k, row, total)
        return total.astype(BF16)

    for target, first, given in ((own_ref, ETA, own_notes), (sent_ref, OFFSET, sent_notes)):
        target[2 * rows :, :] = jnp.zeros((NOTE_ROWS, width), BF16)
        target[2 * rows :, :rows] = notes(first, given)


def pack(trans, covar, inform, offset, eta, count):
    rows, width = trans.shape
    packed = jax.ShapeDtypeStruct((2 * rows + NOTE_ROWS, width), BF16)
    return pl.pallas_call(
        pack_kernel,
        out_shape=(packed, packed),
        in_specs=[VMEM] * 5 + [SMEM],
        out_specs=(VMEM, VMEM),
        name="pack",
    )(trans, covar, inform, offset, eta, count)


def combine_kernel(
    count_ref, trans_ref, covar_ref, offset_ref, notes_ref, inform_hbm, pcovar_hbm, ptrans_hbm, otrans_hbm,
    trans_out, covar_out, offset_out, count_out,
    inform, pcovar, ptrans, otrans, scaled, inner, lead, panel, sems,
):
    rows, width = trans_ref.shape
    strips = width // STRIP
    tall = width // 2
    pairs = ((inform_hbm, inform), (pcovar_hbm, pcovar), (ptrans_hbm, ptrans), (otrans_hbm, otrans))
    copies = [pltpu.make_async_copy(src, dst, sems.at[k]) for k, (src, dst) in enumerate(pairs)]
    for k in (1, 0, 2, 3):
        copies[k].start()

    def note(row):
        return notes_ref[row : row + 1, :]

    count = count_ref[0].astype(F32)
    part_count = note(COUNT)
    has_partner = jnp.max(part_count) > 0.0
    count_out[0] = (jnp.max(part_count) + count).astype(jnp.int32)
    scale = 1.0 / (2.0 + 0.4 * (part_count + count))
    covar_unit = inverse(note(COVAR_GRADE))
    inform_unit = inverse(note(INFORM_GRADE))

    copies[1].wait()
    for part in range(4):
        some = pl.ds(part * (width // 4), width // 4)
        scaled[some, :] = (pcovar[some, :].astype(F32) * inform_unit).astype(BF16)
    copies[0].wait()

    @pl.loop(0, strips)
    def _(s):
        cols = pl.ds(pl.multiple_of(s * STRIP, STRIP), STRIP)
        for half in range(2):
            part = pl.ds(half * tall, tall)
            inner[part, cols] = matmul(scaled[part, :], inform[:, cols]).astype(BF16)

    lead[0] = trans_ref[...].astype(F32)

    @pl.loop(0, 7)
    def _(step):
        now = lax.rem(step, 2)
        panel[0] = (lead[now] * covar_unit).astype(BF16)
        for s in range(strips):
            cols = slice(s * STRIP, (s + 1) * STRIP)
            moved = matmul(panel[0], inner[:, cols])
            rest = lead[now, :, cols]
            value = trans_ref[:, cols].astype(F32) + rest - scale[:, cols] * (rest + moved)
            lead[1 - now, :, cols] = value

    leading = (lead[1] * scale).astype(BF16)
    plain = leading.astype(F32)
    panel[0] = (plain * covar_unit).astype(BF16)
    panel[1] = (plain * inverse(note(TRANS_GRADE))).astype(BF16)
    for s in range(strips):
        cols = slice(s * STRIP, (s + 1) * STRIP)
        panel[2, :, cols] = matmul(panel[0], pcovar[:, cols]).astype(BF16)
    copies[2].wait()
    for s in range(strips):
        cols = slice(s * STRIP, (s + 1) * STRIP)
        moved = matmul(panel[1], ptrans[:, cols]).astype(BF16)
        trans_out[:, cols] = jnp.where(has_partner, moved, trans_ref[:, cols])

    offset_unit = inverse(note(OFFSET_GRADE))
    eta = notes_ref[ETA : ETA + 1, :] * inverse(note(ETA_GRADE))
    row = lax.broadcasted_iota(jnp.int32, (NOTE_ROWS, 1), 0)
    parts = jnp.where((row >= OFFSET) & (row < OFFSET + 3), notes_ref[...] * offset_unit, 0.0)
    etas = jnp.where(row == ETA, jnp.broadcast_to(eta, parts.shape), 0.0)
    moved = times_transpose(parts.astype(BF16), leading) + times_transpose(etas.astype(BF16), panel[2])
    moved = jnp.sum(moved, axis=0, keepdims=True)
    offset_out[...] = jnp.where(has_partner, moved + offset_ref[...], offset_ref[...])

    copies[3].wait()
    own_trans_unit = inverse(note(OWN_TRANS_GRADE))
    for s in range(strips):
        cols = slice(s * STRIP, (s + 1) * STRIP)
        moved = times_transpose(panel[2], otrans[cols, :]) * own_trans_unit[:, cols]
        own = covar_ref[:, cols]
        covar_out[:, cols] = jnp.where(has_partner, (moved + own.astype(F32)).astype(BF16), own)


def combine(count, trans, covar, offset, notes, matrices):
    rows, width = trans.shape
    mat = pltpu.VMEM((width, width), BF16)
    panel = jax.ShapeDtypeStruct((rows, width), BF16)
    return pl.pallas_call(
        combine_kernel,
        out_shape=(
            panel,
            panel,
            jax.ShapeDtypeStruct(offset.shape, F32),
            jax.ShapeDtypeStruct((1,), jnp.int32),
        ),
        in_specs=[SMEM] + [VMEM] * 4 + [ANY] * 4,
        out_specs=(VMEM, VMEM, VMEM, SMEM),
        scratch_shapes=[
            mat, mat, mat, mat, mat, mat,
            pltpu.VMEM((2, rows, width), F32),
            pltpu.VMEM((3, rows, width), BF16),
            pltpu.SemaphoreType.DMA((4,)),
        ],
        compiler_params=pltpu.CompilerParams(vmem_limit_bytes=48 * 2**20),
        name="combine",
    )(count, trans, covar, offset, notes, *matrices)


def fetch_at(distance):

    def fetch(operand):
        sent, own = operand
        devices = range(lax.axis_size("tm"))
        route = [(i - distance, i) for i in devices if i - distance in devices]
        got = lax.ppermute(sent, "tm", route)
        return got, lax.all_gather(own, "state")

    return fetch


def local(transition, covariance, information, offset_vec, info_vec, step_counts, scan_level):
    rows, width = transition.shape[1:]
    trans, covar = transition[0], covariance[0]
    sent, own = pack(trans, covar, information[0], offset_vec, info_vec, step_counts)
    levels = lax.axis_size("tm").bit_length() - 1
    branches = [fetch_at(2**k) for k in range(levels)]
    got, mine = lax.switch(scan_level[0], branches, (sent.astype(F16), own.astype(F16)))
    theirs = lax.all_gather(got, "state")

    def matrix(gathered, place):
        return gathered[:, place * rows : (place + 1) * rows].astype(BF16).reshape(width, width)

    def notes(gathered):
        return gathered[:, 2 * rows :, :rows].astype(F32).transpose(1, 0, 2).reshape(NOTE_ROWS, width)

    matrices = (matrix(mine, 0), matrix(theirs, 0), matrix(theirs, 1), matrix(mine, 1))
    new_trans, new_covariance, new_offset, new_counts = combine(
        step_counts, trans, covar, offset_vec, notes(mine) + notes(theirs), matrices
    )
    return (new_trans[None], new_covariance[None], new_offset, new_counts)


def solution(mesh):
    in_specs = (
        P("tm", "state", None),
        P("tm", "state", None),
        P("tm", "state", None),
        P("tm", "state"),
        P("tm", "state"),
        P("tm"),
        P(),
    )
    out_specs = (P("tm", "state", None), P("tm", "state", None), P("tm", "state"), P("tm"))
    return jax.shard_map(local, mesh=mesh, in_specs=in_specs, out_specs=out_specs, check_vma=False)
```

time: 621 us -> 135 us (0.22)
  the two profiles are of different devices: /device:TPU:1 before, /device:TPU:96 now
where the time goes in v2:
time: 135 us; the launch traced here: 134 us
  blocking collectives  91.5 us (68%)
  Pallas kernels  18.9 us (14%)
  other arithmetic  15.4 us (11%)
  starting transfers between devices  6.39 us (5%)
  between operations  1.97 us (1%)
    all_gather x1, blocking collectives, fetch(): return (got, lax.all_gather(own, 'state'))  46.6 us
    all_gather x1, blocking collectives, local(): theirs = lax.all_gather(got, 'state')  44.9 us
    pallas_call x1, Pallas kernels, combine(): pl.pallas_call(combine_kernel, out_shape=(panel, panel, jax.ShapeDtypeStr...  16.5 us
    convert_element_type x2, other arithmetic, matrix(): gathered[:, place * rows:(place + 1) * rows].astype(BF16)  12.4 us
    ppermute x1, starting transfers between devices, fetch(): got = lax.ppermute(sent, 'tm', route)  6.39 us
  transfers between devices with their start and end apart: 1, of which 0 were waited for; matrix products, arithmetic and copies ran while one was open for 0% of the time, Pallas kernels for 0%

profile of v2, /device:TPU:96, one launch (start us, length us, event | category | flops | bytes accessed | tf_op | source)
XLA Modules:
  0.0 134.4 jit_solution(911626713848427618)
XLA Ops:
  1.3 2.4 %pack.1 = (bf16[176,1280]{1,0:T(8,128)(2,1)}, bf16[176,1280]{1,0:T(8,128)(2,1)}) custom-call(bf16[80,1280]{1,0:T(8,128)(2,1)} %bitcast.15, bf16[80,1280]{1,0:T(8,128)(2,1)} %bitcast.17, bf16[80,1280]{1,0:T(8,128)(2,1)} %bitcast.24, f32[1,80]{1,0:T(1,128)} %offset_ref.3, f32[1,80]{1,0:T(1,128)} %eta_ref.1, s32[1]{0:T(128)S(6)} %copy.22.count_ref), custom_call_target="tpu_custom_call" | custom-call | tf_op jit(solution)/shard_map/pack/pallas_call | solution.py:90
  3.7 1.1 convert_element_type.24
  4.7 1.1 convert_element_type.25
  6.5 53.0 %conditional.1 = (f16[176,1280]{1,0:T(8,128)(2,1)}, f16[2816,1280]{1,0:T(8,128)(2,1)S(1)}) conditional(s32[]{:T(128)} %bitcast.2, (f16[176,1280]{1,0:T(8,128)(2,1)S(1)}, f16[176,1280]{1,0:T(8,128)(2,1)S(1)}) %tuple.28, (f16[176,1280]{1,0:T(8,128)(2,1)S(1)}, f16[176,1280]{1,0:T(8,128)(2,1)S(1)}) %tuple.28, ...), branch_computations={%region_0.0_spmd, %region_1.0_spmd, %region_2.0_spmd, %region_3.0_... | conditional | bytes 9461816 | solution.py:223
  6.5 6.4 %collective-permute-start.2 = (f16[176,1280]{1,0:T(8,128)(2,1)S(1)}, f16[176,1280]{1,0:T(8,128)(2,1)}, u32[]{:S(2)}, u32[]{:S(2)}) collective-permute-start(f16[176,1280]{1,0:T(8,128)(2,1)S(1)} %get-tuple-element.24), channel_id=1, source_target_pairs={{0,64},{16,80},{32,96},{48,112},{64,128},{80,144},{96,160},{112,17... | collective-permute-start | bytes 1351688 | tf_op jit(solution)/shard_map/cond/branch_2_fun/ppermute | solution.py:211
  12.9 46.6 %all-gather.14 = f16[2816,1280]{1,0:T(8,128)(2,1)S(1)} all-gather(f16[176,1280]{1,0:T(8,128)(2,1)S(1)} %get-tuple-element.25), channel_id=4, replica_groups=mesh['tm'=32,'state'=16] {'state'}, dimensions={0}, use_global_device_ids=true | all-gather | bytes 7659520 | tf_op jit(solution)/shard_map/cond/branch_2_fun/all_gather | solution.py:212
  59.5 0.0 collective-permute-done.2
  59.5 0.0 copy-start.3
  59.5 44.9 %all-gather.17 = f16[2816,1280]{1,0:T(8,128)(2,1)} all-gather(f16[176,1280]{1,0:T(8,128)(2,1)} %get-tuple-element.50), channel_id=7, replica_groups=mesh['tm'=32,'state'=16] {'state'}, dimensions={0}, use_global_device_ids=true | all-gather | bytes 7659520 | tf_op jit(solution)/shard_map/all_gather | solution.py:224
  104.4 0.0 copy-done.3
  104.4 0.9 add_bitcast_fusion
  105.4 0.1 add.9.notes_ref
  105.5 6.6 %slice_convert_fusion.1 = (bf16[16,80,1280]{2,1,0:T(8,128)(2,1)}, bf16[16,80,1280]{2,1,0:T(8,128)(2,1)}) fusion(f16[16,176,1280]{2,1,0:T(8,128)(2,1)} %bitcast.5), kind=kLoop, calls=%fused_computation.1 | loop fusion | flops 3276800 | bytes 13107200 | tf_op jit(solution)/shard_map/convert_element_type | solution.py:227
  112.1 0.0 copy-start
  112.1 0.0 copy-start.1
  112.1 0.0 copy-start.2
  112.1 5.8 %slice_convert_fusion = (bf16[16,80,1280]{2,1,0:T(8,128)(2,1)}, bf16[16,80,1280]{2,1,0:T(8,128)(2,1)S(1)}) fusion(f16[16,176,1280]{2,1,0:T(8,128)(2,1)} %bitcast.20), kind=kLoop, calls=%fused_computation | loop fusion | flops 3276800 | bytes 13107200 | tf_op jit(solution)/shard_map/convert_element_type | solution.py:227
  117.8 0.0 copy-done
  117.9 0.0 copy-done.1
  117.9 0.0 copy-done.2
  117.9 16.5 %combine.1 = (bf16[80,1280]{1,0:T(8,128)(2,1)}, bf16[80,1280]{1,0:T(8,128)(2,1)}, f32[1,80]{1,0:T(1,128)}, s32[1]{0:T(128)}) custom-call(s32[1]{0:T(128)S(6)} %copy.22.count_ref, bf16[80,1280]{1,0:T(8,128)(2,1)S(1)} %bitcast.16, bf16[80,1280]{1,0:T(8,128)(2,1)S(1)} %bitcast.18, f32[1,80]{1,0:T(1,128)S(1)} %copy-done.2, f32[16,1280]{1,0:T(8,128)S(1)} %add.9.notes_ref, ...), custom_call_target="tpu_custom_call" | custom-call | tf_op jit(solution)/shard_map/combine/pallas_call | solution.py:184
  (1 shorter events, 0.0 us)
Async XLA Ops:
  6.5 53.0 %collective-permute-start.2 = (f16[176,1280]{1,0:T(8,128)(2,1)S(1)}, f16[176,1280]{1,0:T(8,128)(2,1)}, u32[]{:S(2)}, u32[]{:S(2)}) collective-permute-start(f16[176,1280]{1,0:T(8,128)(2,1)S(1)} %get-tuple-element.24), channel_id=1, source_target_pairs={{0,64},{16,80},{32,96},{48,112},{64,128},{80,144},{96,160},{112,17... | collective-permute-start | bytes 1351688 | tf_op jit(solution)/shard_map/cond/branch_2_fun/ppermute | solution.py:211
  59.5 44.9 %copy-start.3 = (f16[2816,1280]{1,0:T(8,128)(2,1)}, f16[2816,1280]{1,0:T(8,128)(2,1)S(1)}, u32[]{:S(2)}) copy-start(f16[2816,1280]{1,0:T(8,128)(2,1)S(1)} %get-tuple-element.51) | copy-start | bytes 21626884
  112.1 5.8 %copy-start = (bf16[1,80,1280]{2,1,0:T(8,128)(2,1)S(1)}, bf16[1,80,1280]{2,1,0:T(8,128)(2,1)}, u32[]{:S(2)}) copy-start(bf16[1,80,1280]{2,1,0:T(8,128)(2,1)} %param.12) | copy-start | bytes 614404
  112.1 5.8 %copy-start.1 = (bf16[1,80,1280]{2,1,0:T(8,128)(2,1)S(1)}, bf16[1,80,1280]{2,1,0:T(8,128)(2,1)}, u32[]{:S(2)}) copy-start(bf16[1,80,1280]{2,1,0:T(8,128)(2,1)} %param.13) | copy-start | bytes 614404
  112.1 5.8 %copy-start.2 = (f32[1,80]{1,0:T(1,128)S(1)}, f32[1,80]{1,0:T(1,128)}, u32[]{:S(2)}) copy-start(f32[1,80]{1,0:T(1,128)} %offset_ref.3) | copy-start | bytes 964

commit v3 on v2

--- a/solution.py
+++ b/solution.py
@@ -6,13 +6,14 @@
 from jax.sharding import PartitionSpec as P
 
 F32, BF16, F16 = jnp.float32, jnp.bfloat16, jnp.float16
-NOTE_ROWS = 16
+NOTE_ROWS = 8
+ALL_NOTES = 2 * NOTE_ROWS
 STRIP = 256
 BASE = 2.0**12
 STEP = 2.0**16
 STEPS = 7
 ETA, ETA_GRADE, INFORM_GRADE, OWN_TRANS_GRADE = 0, 1, 2, 3
-OFFSET, OFFSET_GRADE, COVAR_GRADE, TRANS_GRADE, COUNT = 4, 7, 8, 9, 10
+OFFSET, OFFSET_GRADE, COVAR_GRADE, TRANS_GRADE, COUNT = 8, 11, 12, 13, 14
 
 VMEM = pl.BlockSpec(memory_space=pltpu.VMEM)
 SMEM = pl.BlockSpec(memory_space=pltpu.SMEM)
@@ -44,7 +45,7 @@
     return factor
 
 
-def pack_kernel(trans_ref, covar_ref, inform_ref, offset_ref, eta_ref, count_ref, sent_ref, own_ref):
+def pack_kernel(trans_ref, covar_ref, inform_ref, offset_ref, eta_ref, count_ref, sent_ref, own_ref, notes_ref):
     rows, width = trans_ref.shape
 
     def put(target, first, value_ref):
@@ -72,42 +73,41 @@
     count = one * count_ref[0].astype(F32)
     sent_notes = parts + [one * offset_grade, covar_grade, trans_grade, count]
 
-    def notes(first, given):
-        index = lax.broadcasted_iota(jnp.int32, (NOTE_ROWS, rows), 0)
-        total = jnp.zeros((NOTE_ROWS, rows), F32)
+    index = lax.broadcasted_iota(jnp.int32, (ALL_NOTES, rows), 0)
+    total = jnp.zeros((ALL_NOTES, rows), F32)
+    for first, given in ((ETA, own_notes), (OFFSET, sent_notes)):
         for k, row in enumerate(given):
             total = jnp.where(index == first + k, row, total)
-        return total.astype(BF16)
-
-    for target, first, given in ((own_ref, ETA, own_notes), (sent_ref, OFFSET, sent_notes)):
-        target[2 * rows :, :] = jnp.zeros((NOTE_ROWS, width), BF16)
-        target[2 * rows :, :rows] = notes(first, given)
+    notes_ref[...] = jnp.zeros((ALL_NOTES, width), BF16)
+    notes_ref[:, :rows] = total.astype(BF16)
 
 
 def pack(trans, covar, inform, offset, eta, count):
     rows, width = trans.shape
-    packed = jax.ShapeDtypeStruct((2 * rows + NOTE_ROWS, width), BF16)
+    packed = jax.ShapeDtypeStruct((2 * rows, width), BF16)
     return pl.pallas_call(
         pack_kernel,
-        out_shape=(packed, packed),
+        out_shape=(packed, packed, jax.ShapeDtypeStruct((ALL_NOTES, width), BF16)),
         in_specs=[VMEM] * 5 + [SMEM],
-        out_specs=(VMEM, VMEM),
+        out_specs=(VMEM, VMEM, VMEM),
         name="pack",
     )(trans, covar, inform, offset, eta, count)
 
 
 def combine_kernel(
-    count_ref, trans_ref, covar_ref, offset_ref, notes_ref, inform_hbm, pcovar_hbm, ptrans_hbm, otrans_hbm,
+    count_ref, trans_ref, covar_ref, offset_ref, notes_ref, inform, pcovar, ptrans_hbm, otrans_hbm,
     trans_out, covar_out, offset_out, count_out,
-    inform, pcovar, ptrans, otrans, scaled, inner, lead, panel, sems,
+    ptrans, otrans, scaled, inner, lead, panel, sems,
 ):
     rows, width = trans_ref.shape
     strips = width // STRIP
     tall = width // 2
-    pairs = ((inform_hbm, inform), (pcovar_hbm, pcovar), (ptrans_hbm, ptrans), (otrans_hbm, otrans))
-    copies = [pltpu.make_async_copy(src, dst, sems.at[k]) for k, (src, dst) in enumerate(pairs)]
-    for k in (1, 0, 2, 3):
-        copies[k].start()
+    copies = [
+        pltpu.make_async_copy(ptrans_hbm, ptrans, sems.at[0]),
+        pltpu.make_async_copy(otrans_hbm, otrans, sems.at[1]),
+    ]
+    for copy in copies:
+        copy.start()
 
     def note(row):
         return notes_ref[row : row + 1, :]
@@ -120,11 +120,9 @@
     covar_unit = inverse(note(COVAR_GRADE))
     inform_unit = inverse(note(INFORM_GRADE))
 
-    copies[1].wait()
     for part in range(4):
         some = pl.ds(part * (width // 4), width // 4)
         scaled[some, :] = (pcovar[some, :].astype(F32) * inform_unit).astype(BF16)
-    copies[0].wait()
 
     @pl.loop(0, strips)
     def _(s):
@@ -153,7 +151,7 @@
     for s in range(strips):
         cols = slice(s * STRIP, (s + 1) * STRIP)
         panel[2, :, cols] = matmul(panel[0], pcovar[:, cols]).astype(BF16)
-    copies[2].wait()
+    copies[0].wait()
     for s in range(strips):
         cols = slice(s * STRIP, (s + 1) * STRIP)
         moved = matmul(panel[1], ptrans[:, cols]).astype(BF16)
@@ -161,14 +159,14 @@
 
     offset_unit = inverse(note(OFFSET_GRADE))
     eta = notes_ref[ETA : ETA + 1, :] * inverse(note(ETA_GRADE))
-    row = lax.broadcasted_iota(jnp.int32, (NOTE_ROWS, 1), 0)
+    row = lax.broadcasted_iota(jnp.int32, (ALL_NOTES, 1), 0)
     parts = jnp.where((row >= OFFSET) & (row < OFFSET + 3), notes_ref[...] * offset_unit, 0.0)
     etas = jnp.where(row == ETA, jnp.broadcast_to(eta, parts.shape), 0.0)
     moved = times_transpose(parts.astype(BF16), leading) + times_transpose(etas.astype(BF16), panel[2])
     moved = jnp.sum(moved, axis=0, keepdims=True)
     offset_out[...] = jnp.where(has_partner, moved + offset_ref[...], offset_ref[...])
 
-    copies[3].wait()
+    copies[1].wait()
     own_trans_unit = inverse(note(OWN_TRANS_GRADE))
     for s in range(strips):
         cols = slice(s * STRIP, (s + 1) * STRIP)
@@ -189,13 +187,13 @@
             jax.ShapeDtypeStruct(offset.shape, F32),
             jax.ShapeDtypeStruct((1,), jnp.int32),
         ),
-        in_specs=[SMEM] + [VMEM] * 4 + [ANY] * 4,
+        in_specs=[SMEM] + [VMEM] * 6 + [ANY] * 2,
         out_specs=(VMEM, VMEM, VMEM, SMEM),
         scratch_shapes=[
-            mat, mat, mat, mat, mat, mat,
+            mat, mat, mat, mat,
             pltpu.VMEM((2, rows, width), F32),
             pltpu.VMEM((3, rows, width), BF16),
-            pltpu.SemaphoreType.DMA((4,)),
+            pltpu.SemaphoreType.DMA((2,)),
         ],
         compiler_params=pltpu.CompilerParams(vmem_limit_bytes=48 * 2**20),
         name="combine",
@@ -217,10 +215,12 @@
 def local(transition, covariance, information, offset_vec, info_vec, step_counts, scan_level):
     rows, width = transition.shape[1:]
     trans, covar = transition[0], covariance[0]
-    sent, own = pack(trans, covar, information[0], offset_vec, info_vec, step_counts)
+    sent, own, own_notes = pack(trans, covar, information[0], offset_vec, info_vec, step_counts)
+    sent = jnp.concatenate([sent, own_notes[NOTE_ROWS:]]).astype(F16)
+    own = jnp.concatenate([own, own_notes[:NOTE_ROWS]]).astype(F16)
     levels = lax.axis_size("tm").bit_length() - 1
     branches = [fetch_at(2**k) for k in range(levels)]
-    got, mine = lax.switch(scan_level[0], branches, (sent.astype(F16), own.astype(F16)))
+    got, mine = lax.switch(scan_level[0], branches, (sent, own))
     theirs = lax.all_gather(got, "state")
 
     def matrix(gathered, place):
@@ -231,7 +231,7 @@
 
     matrices = (matrix(mine, 0), matrix(theirs, 0), matrix(theirs, 1), matrix(mine, 1))
     new_trans, new_covariance, new_offset, new_counts = combine(
-        step_counts, trans, covar, offset_vec, notes(mine) + notes(theirs), matrices
+        step_counts, trans, covar, offset_vec, jnp.concatenate([notes(mine), notes(theirs)]), matrices
     )
     return (new_trans[None], new_covariance[None], new_offset, new_counts)
 

time: 135 us -> 132 us (0.978)
  the two profiles are of different devices: /device:TPU:96 before, /device:TPU:128 now
where the time goes in v3:
time: 132 us; the launch traced here: 133 us
  blocking collectives  87.5 us (66%)
  Pallas kernels  19.4 us (15%)
  other arithmetic  11.6 us (9%)
  starting transfers between devices  9.1 us (7%)
  local copies, waits for them, and re-layouts  3.31 us (3%)
  between operations  1.99 us (2%)
    all_gather x1, blocking collectives, fetch(): return (got, lax.all_gather(own, 'state'))  46 us
    all_gather x1, blocking collectives, local(): theirs = lax.all_gather(got, 'state')  41.5 us
    pallas_call x1, Pallas kernels, combine(): pl.pallas_call(combine_kernel, out_shape=(panel, panel, jax.ShapeDtypeStr...  17.1 us
    convert_element_type x2, other arithmetic, matrix(): gathered[:, place * rows:(place + 1) * rows].astype(BF16)  9.63 us
    ppermute x1, starting transfers between devices, fetch(): got = lax.ppermute(sent, 'tm', route)  9.1 us
  transfers between devices with their start and end apart: 1, of which 0 were waited for; matrix products, arithmetic and copies ran while one was open for 0% of the time, Pallas kernels for 0%

profile of v3, /device:TPU:128, one launch (start us, length us, event | category | flops | bytes accessed | tf_op | source)
XLA Modules:
  0.0 133.1 jit_solution(6644355699291745013)
XLA Ops:
  1.9 2.3 %pack.1 = (bf16[160,1280]{1,0:T(8,128)(2,1)}, bf16[160,1280]{1,0:T(8,128)(2,1)}, bf16[16,1280]{1,0:T(8,128)(2,1)}) custom-call(bf16[80,1280]{1,0:T(8,128)(2,1)} %bitcast.17, bf16[80,1280]{1,0:T(8,128)(2,1)} %bitcast.19, bf16[80,1280]{1,0:T(8,128)(2,1)} %bitcast.26, f32[1,80]{1,0:T(1,128)} %offset_ref.3, f32[1,80]{1,0:T(1,128)} %eta_ref.1, s32[1]{0:T(128)S(6)} %copy.23.count_ref), custom_call_target="tpu_custom_call" | custom-call | tf_op jit(solution)/shard_map/pack/pallas_call | solution.py:88
  4.3 0.7 fusion
  5.0 1.3 maximum_convert_fusion
  6.3 55.2 %conditional.1 = (f16[168,1280]{1,0:T(8,128)(2,1)}, f16[2688,1280]{1,0:T(8,128)(2,1)}) conditional(s32[]{:T(128)} %bitcast.2, (f16[168,1280]{1,0:T(8,128)(2,1)S(1)}, f16[168,1280]{1,0:T(8,128)(2,1)S(1)}) %maximum_convert_fusion, (f16[168,1280]{1,0:T(8,128)(2,1)S(1)}, ...), branch_computations={%region_0.0_spmd, %region_1.0_spmd, %region_2.0_spmd, %region_3.0_... | conditional | bytes 9031736 | solution.py:223
  6.3 9.1 %collective-permute-start.3 = (f16[168,1280]{1,0:T(8,128)(2,1)S(1)}, f16[168,1280]{1,0:T(8,128)(2,1)}, u32[]{:S(2)}, u32[]{:S(2)}) collective-permute-start(f16[168,1280]{1,0:T(8,128)(2,1)S(1)} %get-tuple-element.26), channel_id=1, source_target_pairs={{0,128},{16,144},{32,160},{48,176},{64,192},{80,208},{96,224},{112... | collective-permute-start | bytes 1290248 | tf_op jit(solution)/shard_map/cond/branch_3_fun/ppermute | solution.py:209
  15.4 46.0 %all-gather.15 = f16[2688,1280]{1,0:T(8,128)(2,1)} all-gather(f16[168,1280]{1,0:T(8,128)(2,1)S(1)} %get-tuple-element.27), channel_id=5, replica_groups=mesh['tm'=32,'state'=16] {'state'}, dimensions={0}, use_global_device_ids=true | all-gather | bytes 7311360 | tf_op jit(solution)/shard_map/cond/branch_3_fun/all_gather | solution.py:210
  61.4 0.0 collective-permute-done.3
  61.5 0.8 slice_bitcast_fusion.1
  62.2 5.7 %slice_convert_fusion = (bf16[16,80,1280]{2,1,0:T(8,128)(2,1)}, bf16[16,80,1280]{2,1,0:T(8,128)(2,1)S(1)}) fusion(f16[16,168,1280]{2,1,0:T(8,128)(2,1)} %bitcast.4), kind=kLoop, calls=%fused_computation | loop fusion | flops 3276800 | bytes 13107200 | tf_op jit(solution)/shard_map/convert_element_type | solution.py:227
  67.9 0.1 reshape.31
  68.1 41.5 %all-gather.17 = f16[2688,1280]{1,0:T(8,128)(2,1)S(1)} all-gather(f16[168,1280]{1,0:T(8,128)(2,1)} %get-tuple-element.52), channel_id=7, replica_groups=mesh['tm'=32,'state'=16] {'state'}, dimensions={0}, use_global_device_ids=true | all-gather | bytes 7311360 | tf_op jit(solution)/shard_map/all_gather | solution.py:224
  109.6 0.0 copy-start
  109.6 0.0 copy-start.2
  109.6 3.9 %slice_convert_fusion.1 = (bf16[16,80,1280]{2,1,0:T(8,128)(2,1)}, bf16[16,80,1280]{2,1,0:T(8,128)(2,1)}) fusion(f16[16,168,1280]{2,1,0:T(8,128)(2,1)S(1)} %bitcast.22), kind=kLoop, calls=%fused_computation.1 | loop fusion | flops 3276800 | bytes 13107200 | tf_op jit(solution)/shard_map/convert_element_type | solution.py:227
  113.6 0.7 reshape.32
  114.3 0.7 maximum_convert_fusion.2.notes_ref
  115.0 0.0 copy-done
  115.0 0.0 copy-done.2
  115.0 0.0 copy-start.1
  115.0 0.9 copy-done.1
  116.0 17.1 %combine.1 = (bf16[80,1280]{1,0:T(8,128)(2,1)}, bf16[80,1280]{1,0:T(8,128)(2,1)}, f32[1,80]{1,0:T(1,128)}, s32[1]{0:T(128)}) custom-call(s32[1]{0:T(128)S(6)} %copy.23.count_ref, bf16[80,1280]{1,0:T(8,128)(2,1)S(1)} %bitcast.18, bf16[80,1280]{1,0:T(8,128)(2,1)S(1)} %bitcast.20, f32[1,80]{1,0:T(1,128)S(1)} %copy-done.2, ...), custom_call_target="tpu_custom_call" | custom-call | tf_op jit(solution)/shard_map/combine/pallas_call | solution.py:182
  (3 shorter events, 0.0 us)
Async XLA Ops:
  6.3 55.1 %collective-permute-start.3 = (f16[168,1280]{1,0:T(8,128)(2,1)S(1)}, f16[168,1280]{1,0:T(8,128)(2,1)}, u32[]{:S(2)}, u32[]{:S(2)}) collective-permute-start(f16[168,1280]{1,0:T(8,128)(2,1)S(1)} %get-tuple-element.26), channel_id=1, source_target_pairs={{0,128},{16,144},{32,160},{48,176},{64,192},{80,208},{96,224},{112... | collective-permute-start | bytes 1290248 | tf_op jit(solution)/shard_map/cond/branch_3_fun/ppermute | solution.py:209
  109.6 5.4 %copy-start = (bf16[1,80,1280]{2,1,0:T(8,128)(2,1)S(1)}, bf16[1,80,1280]{2,1,0:T(8,128)(2,1)}, u32[]{:S(2)}) copy-start(bf16[1,80,1280]{2,1,0:T(8,128)(2,1)} %param.12) | copy-start | bytes 614404
  109.6 5.4 %copy-start.2 = (f32[1,80]{1,0:T(1,128)S(1)}, f32[1,80]{1,0:T(1,128)}, u32[]{:S(2)}) copy-start(f32[1,80]{1,0:T(1,128)} %offset_ref.3) | copy-start | bytes 964
  115.0 0.9 copy-start.1

commit v4 on v2

--- a/solution.py
+++ b/solution.py
@@ -6,13 +6,14 @@
 from jax.sharding import PartitionSpec as P
 
 F32, BF16, F16 = jnp.float32, jnp.bfloat16, jnp.float16
-NOTE_ROWS = 16
+NOTE_ROWS = 8
+PACKED_ROWS = 16
 STRIP = 256
 BASE = 2.0**12
 STEP = 2.0**16
 STEPS = 7
 ETA, ETA_GRADE, INFORM_GRADE, OWN_TRANS_GRADE = 0, 1, 2, 3
-OFFSET, OFFSET_GRADE, COVAR_GRADE, TRANS_GRADE, COUNT = 4, 7, 8, 9, 10
+OFFSET_GRADE, COVAR_GRADE, TRANS_GRADE, COUNT = 3, 4, 5, 6
 
 VMEM = pl.BlockSpec(memory_space=pltpu.VMEM)
 SMEM = pl.BlockSpec(memory_space=pltpu.SMEM)
@@ -72,21 +73,18 @@
     count = one * count_ref[0].astype(F32)
     sent_notes = parts + [one * offset_grade, covar_grade, trans_grade, count]
 
-    def notes(first, given):
-        index = lax.broadcasted_iota(jnp.int32, (NOTE_ROWS, rows), 0)
-        total = jnp.zeros((NOTE_ROWS, rows), F32)
+    index = lax.broadcasted_iota(jnp.int32, (PACKED_ROWS, rows), 0)
+    for target, given in ((own_ref, own_notes), (sent_ref, sent_notes)):
+        total = jnp.zeros((PACKED_ROWS, rows), F32)
         for k, row in enumerate(given):
-            total = jnp.where(index == first + k, row, total)
-        return total.astype(BF16)
-
-    for target, first, given in ((own_ref, ETA, own_notes), (sent_ref, OFFSET, sent_notes)):
-        target[2 * rows :, :] = jnp.zeros((NOTE_ROWS, width), BF16)
-        target[2 * rows :, :rows] = notes(first, given)
+            total = jnp.where(index == k, row, total)
+        target[2 * rows :, :] = jnp.zeros((PACKED_ROWS, width), BF16)
+        target[2 * rows :, :rows] = total.astype(BF16)
 
 
 def pack(trans, covar, inform, offset, eta, count):
     rows, width = trans.shape
-    packed = jax.ShapeDtypeStruct((2 * rows + NOTE_ROWS, width), BF16)
+    packed = jax.ShapeDtypeStruct((2 * rows + PACKED_ROWS, width), BF16)
     return pl.pallas_call(
         pack_kernel,
         out_shape=(packed, packed),
@@ -97,20 +95,24 @@
 
 
 def combine_kernel(
-    count_ref, trans_ref, covar_ref, offset_ref, notes_ref, inform_hbm, pcovar_hbm, ptrans_hbm, otrans_hbm,
+    count_ref, trans_ref, covar_ref, offset_ref, both_ref,
+    inform_hbm, pcovar_hbm, ptrans_hbm, otrans_hbm,
     trans_out, covar_out, offset_out, count_out,
     inform, pcovar, ptrans, otrans, scaled, inner, lead, panel, sems,
 ):
     rows, width = trans_ref.shape
     strips = width // STRIP
     tall = width // 2
-    pairs = ((inform_hbm, inform), (pcovar_hbm, pcovar), (ptrans_hbm, ptrans), (otrans_hbm, otrans))
+    pairs = ((pcovar_hbm, pcovar), (inform_hbm, inform), (ptrans_hbm, ptrans), (otrans_hbm, otrans))
     copies = [pltpu.make_async_copy(src, dst, sems.at[k]) for k, (src, dst) in enumerate(pairs)]
-    for k in (1, 0, 2, 3):
-        copies[k].start()
+    for copy in copies:
+        copy.start()
+
+    def own_note(row):
+        return both_ref[row : row + 1, :]
 
     def note(row):
-        return notes_ref[row : row + 1, :]
+        return both_ref[NOTE_ROWS + row : NOTE_ROWS + row + 1, :]
 
     count = count_ref[0].astype(F32)
     part_count = note(COUNT)
@@ -118,13 +120,14 @@
     count_out[0] = (jnp.max(part_count) + count).astype(jnp.int32)
     scale = 1.0 / (2.0 + 0.4 * (part_count + count))
     covar_unit = inverse(note(COVAR_GRADE))
-    inform_unit = inverse(note(INFORM_GRADE))
-
-    copies[1].wait()
+    inform_unit = inverse(own_note(INFORM_GRADE))
+
+    copies[0].wait()
     for part in range(4):
         some = pl.ds(part * (width // 4), width // 4)
         scaled[some, :] = (pcovar[some, :].astype(F32) * inform_unit).astype(BF16)
-    copies[0].wait()
+
+    copies[1].wait()
 
     @pl.loop(0, strips)
     def _(s):
@@ -160,16 +163,18 @@
         trans_out[:, cols] = jnp.where(has_partner, moved, trans_ref[:, cols])
 
     offset_unit = inverse(note(OFFSET_GRADE))
-    eta = notes_ref[ETA : ETA + 1, :] * inverse(note(ETA_GRADE))
+    eta = own_note(ETA) * inverse(own_note(ETA_GRADE))
     row = lax.broadcasted_iota(jnp.int32, (NOTE_ROWS, 1), 0)
-    parts = jnp.where((row >= OFFSET) & (row < OFFSET + 3), notes_ref[...] * offset_unit, 0.0)
-    etas = jnp.where(row == ETA, jnp.broadcast_to(eta, parts.shape), 0.0)
-    moved = times_transpose(parts.astype(BF16), leading) + times_transpose(etas.astype(BF16), panel[2])
+    parts = jnp.where(row < OFFSET_GRADE, both_ref[NOTE_ROWS:, :] * offset_unit, 0.0)
+    etas = jnp.where(row == 0, jnp.broadcast_to(eta, parts.shape), 0.0)
+    nothing = jnp.zeros(parts.shape, F32)
+    moved = times_transpose(jnp.concatenate([parts, nothing]).astype(BF16), leading)
+    moved += times_transpose(jnp.concatenate([etas, nothing]).astype(BF16), panel[2])
     moved = jnp.sum(moved, axis=0, keepdims=True)
     offset_out[...] = jnp.where(has_partner, moved + offset_ref[...], offset_ref[...])
 
     copies[3].wait()
-    own_trans_unit = inverse(note(OWN_TRANS_GRADE))
+    own_trans_unit = inverse(own_note(OWN_TRANS_GRADE))
     for s in range(strips):
         cols = slice(s * STRIP, (s + 1) * STRIP)
         moved = times_transpose(panel[2], otrans[cols, :]) * own_trans_unit[:, cols]
@@ -177,7 +182,7 @@
         covar_out[:, cols] = jnp.where(has_partner, (moved + own.astype(F32)).astype(BF16), own)
 
 
-def combine(count, trans, covar, offset, notes, matrices):
+def combine(count, trans, covar, offset, both, matrices):
     rows, width = trans.shape
     mat = pltpu.VMEM((width, width), BF16)
     panel = jax.ShapeDtypeStruct((rows, width), BF16)
@@ -199,7 +204,7 @@
         ],
         compiler_params=pltpu.CompilerParams(vmem_limit_bytes=48 * 2**20),
         name="combine",
-    )(count, trans, covar, offset, notes, *matrices)
+    )(count, trans, covar, offset, both, *matrices)
 
 
 def fetch_at(distance):
@@ -218,9 +223,11 @@
     rows, width = transition.shape[1:]
     trans, covar = transition[0], covariance[0]
     sent, own = pack(trans, covar, information[0], offset_vec, info_vec, step_counts)
+    kept = 2 * rows + NOTE_ROWS
+    sent, own = sent[:kept].astype(F16), own[:kept].astype(F16)
     levels = lax.axis_size("tm").bit_length() - 1
     branches = [fetch_at(2**k) for k in range(levels)]
-    got, mine = lax.switch(scan_level[0], branches, (sent.astype(F16), own.astype(F16)))
+    got, mine = lax.switch(scan_level[0], branches, (sent, own))
     theirs = lax.all_gather(got, "state")
 
     def matrix(gathered, place):
@@ -231,7 +238,7 @@
 
     matrices = (matrix(mine, 0), matrix(theirs, 0), matrix(theirs, 1), matrix(mine, 1))
     new_trans, new_covariance, new_offset, new_counts = combine(
-        step_counts, trans, covar, offset_vec, notes(mine) + notes(theirs), matrices
+        step_counts, trans, covar, offset_vec, jnp.concatenate([notes(mine), notes(theirs)]), matrices
     )
     return (new_trans[None], new_covariance[None], new_offset, new_counts)
 

time: 135 us -> 128 us (0.948)
  the two profiles are of different devices: /device:TPU:96 before, /device:TPU:224 now
where the time goes in v4:
time: 128 us; the launch traced here: 126 us
  blocking collectives  85.7 us (67%)
  Pallas kernels  18.9 us (15%)
  other arithmetic  11.7 us (9%)
  starting transfers between devices  5.04 us (4%)
  local copies, waits for them, and re-layouts  2.56 us (2%)
  between operations  1.98 us (2%)
    all_gather x1, blocking collectives, fetch(): return (got, lax.all_gather(own, 'state'))  45.9 us
    all_gather x1, blocking collectives, local(): theirs = lax.all_gather(got, 'state')  39.8 us
    pallas_call x1, Pallas kernels, combine(): pl.pallas_call(combine_kernel, out_shape=(panel, panel, jax.ShapeDtypeStr...  16.5 us
    convert_element_type x2, other arithmetic, matrix(): gathered[:, place * rows:(place + 1) * rows].astype(BF16)  9.63 us
    ppermute x1, starting transfers between devices, fetch(): got = lax.ppermute(sent, 'tm', route)  5.04 us
  transfers between devices with their start and end apart: 1, of which 0 were waited for; matrix products, arithmetic and copies ran while one was open for 0% of the time, Pallas kernels for 0%

profile of v4, /device:TPU:224, one launch (start us, length us, event | category | flops | bytes accessed | tf_op | source)
XLA Modules:
  0.0 125.8 jit_solution(3929231416517270648)
XLA Ops:
  1.9 2.4 %pack.1 = (bf16[176,1280]{1,0:T(8,128)(2,1)}, bf16[176,1280]{1,0:T(8,128)(2,1)}) custom-call(bf16[80,1280]{1,0:T(8,128)(2,1)} %bitcast.17, bf16[80,1280]{1,0:T(8,128)(2,1)} %bitcast.19, bf16[80,1280]{1,0:T(8,128)(2,1)} %bitcast.26, f32[1,80]{1,0:T(1,128)} %offset_ref.3, f32[1,80]{1,0:T(1,128)} %eta_ref.1, s32[1]{0:T(128)S(6)} %copy.23.count_ref), custom_call_target="tpu_custom_call" | custom-call | tf_op jit(solution)/shard_map/pack/pallas_call | solution.py:88
  4.3 1.3 %slice_convert_fusion.4 = (f16[168,1280]{1,0:T(8,128)(2,1)S(1)}, f16[168,1280]{1,0:T(8,128)(2,1)S(1)}) fusion(bf16[176,1280]{1,0:T(8,128)(2,1)} %get-tuple-element.43, bf16[176,1280]{1,0:T(8,128)(2,1)} %get-tuple-element.42), kind=kLoop, calls=%fused_computation.4 | loop fusion | flops 430080 | bytes 1720320 | tf_op jit(solution)/shard_map/convert_element_type | solution.py:227
  5.6 51.0 %conditional.1 = (f16[168,1280]{1,0:T(8,128)(2,1)}, f16[2688,1280]{1,0:T(8,128)(2,1)}) conditional(s32[]{:T(128)} %bitcast.2, (f16[168,1280]{1,0:T(8,128)(2,1)S(1)}, f16[168,1280]{1,0:T(8,128)(2,1)S(1)}) %tuple.28, (f16[168,1280]{1,0:T(8,128)(2,1)S(1)}, f16[168,1280]{1,0:T(8,128)(2,1)S(1)}) %tuple.28, ...), branch_computations={%region_0.0_spmd, %region_1.0_spmd, %region_2.0_spmd, %region_3.0_... | conditional | bytes 9031736 | solution.py:230
  5.6 5.0 %collective-permute-start.1 = (f16[168,1280]{1,0:T(8,128)(2,1)S(1)}, f16[168,1280]{1,0:T(8,128)(2,1)}, u32[]{:S(2)}, u32[]{:S(2)}) collective-permute-start(f16[168,1280]{1,0:T(8,128)(2,1)S(1)} %get-tuple-element.22), channel_id=1, source_target_pairs={{0,32},{16,48},{32,64},{48,80},{64,96},{80,112},{96,128},{112,144}... | collective-permute-start | bytes 1290248 | tf_op jit(solution)/shard_map/cond/branch_1_fun/ppermute | solution.py:216
  10.7 45.9 %all-gather.13 = f16[2688,1280]{1,0:T(8,128)(2,1)} all-gather(f16[168,1280]{1,0:T(8,128)(2,1)S(1)} %get-tuple-element.23), channel_id=3, replica_groups=mesh['tm'=32,'state'=16] {'state'}, dimensions={0}, use_global_device_ids=true | all-gather | bytes 7311360 | tf_op jit(solution)/shard_map/cond/branch_1_fun/all_gather | solution.py:217
  56.6 0.0 collective-permute-done.1
  56.6 0.8 slice_bitcast_fusion.1
  57.4 5.7 %slice_convert_fusion = (bf16[16,80,1280]{2,1,0:T(8,128)(2,1)}, bf16[16,80,1280]{2,1,0:T(8,128)(2,1)S(1)}) fusion(f16[16,168,1280]{2,1,0:T(8,128)(2,1)} %bitcast.4), kind=kLoop, calls=%fused_computation | loop fusion | flops 3276800 | bytes 13107200 | tf_op jit(solution)/shard_map/convert_element_type | solution.py:234
  63.1 0.1 reshape.31
  63.2 39.8 %all-gather.17 = f16[2688,1280]{1,0:T(8,128)(2,1)S(1)} all-gather(f16[168,1280]{1,0:T(8,128)(2,1)} %get-tuple-element.50), channel_id=7, replica_groups=mesh['tm'=32,'state'=16] {'state'}, dimensions={0}, use_global_device_ids=true | all-gather | bytes 7311360 | tf_op jit(solution)/shard_map/all_gather | solution.py:231
  103.0 0.0 copy-start
  103.0 0.0 copy-start.2
  103.0 3.9 %slice_convert_fusion.1 = (bf16[16,80,1280]{2,1,0:T(8,128)(2,1)}, bf16[16,80,1280]{2,1,0:T(8,128)(2,1)}) fusion(f16[16,168,1280]{2,1,0:T(8,128)(2,1)S(1)} %bitcast.22), kind=kLoop, calls=%fused_computation.1 | loop fusion | flops 3276800 | bytes 13107200 | tf_op jit(solution)/shard_map/convert_element_type | solution.py:234
  106.9 0.7 reshape.32
  107.6 0.7 maximum_convert_fusion.both_ref
  108.4 0.0 copy-done
  108.4 0.0 copy-done.2
  108.4 0.0 copy-start.1
  108.4 0.9 copy-done.1
  109.3 16.5 %combine.1 = (bf16[80,1280]{1,0:T(8,128)(2,1)}, bf16[80,1280]{1,0:T(8,128)(2,1)}, f32[1,80]{1,0:T(1,128)}, s32[1]{0:T(128)}) custom-call(s32[1]{0:T(128)S(6)} %copy.23.count_ref, bf16[80,1280]{1,0:T(8,128)(2,1)S(1)} %bitcast.18, bf16[80,1280]{1,0:T(8,128)(2,1)S(1)} %bitcast.20, f32[1,80]{1,0:T(1,128)S(1)} %copy-done.2, ...), custom_call_target="tpu_custom_call" | custom-call | tf_op jit(solution)/shard_map/combine/pallas_call | solution.py:189
  (3 shorter events, 0.0 us)
Async XLA Ops:
  5.6 51.0 %collective-permute-start.1 = (f16[168,1280]{1,0:T(8,128)(2,1)S(1)}, f16[168,1280]{1,0:T(8,128)(2,1)}, u32[]{:S(2)}, u32[]{:S(2)}) collective-permute-start(f16[168,1280]{1,0:T(8,128)(2,1)S(1)} %get-tuple-element.22), channel_id=1, source_target_pairs={{0,32},{16,48},{32,64},{48,80},{64,96},{80,112},{96,128},{112,144}... | collective-permute-start | bytes 1290248 | tf_op jit(solution)/shard_map/cond/branch_1_fun/ppermute | solution.py:216
  103.0 5.4 %copy-start = (bf16[1,80,1280]{2,1,0:T(8,128)(2,1)S(1)}, bf16[1,80,1280]{2,1,0:T(8,128)(2,1)}, u32[]{:S(2)}) copy-start(bf16[1,80,1280]{2,1,0:T(8,128)(2,1)} %param.12) | copy-start | bytes 614404
  103.0 5.4 %copy-start.2 = (f32[1,80]{1,0:T(1,128)S(1)}, f32[1,80]{1,0:T(1,128)}, u32[]{:S(2)}) copy-start(f32[1,80]{1,0:T(1,128)} %offset_ref.3) | copy-start | bytes 964
  108.4 0.9 copy-start.1
